TPU v7x, 32 devices: a whole 2x2x4 slice. The times are simulated.
32 devices in a mesh: groups: 2 (over y), lat: 8 (over z, core), row: 2 (over x).
Axes of the slice: x: 2, y: 2, z: 4, core: 2. Of those that a mesh axis runs over, the one named last changes fastest.
Arguments:
- stream_rows: bfloat16 [2048, 4096], P(('groups', 'lat'), 'row'), parts along dimension 0, may hold values from -6 to 6
- active_blocks: int32 [2048, 3], P(('groups', 'lat')), parts along dimension 0, may hold values from 0 to 7, all different within a row; in each aligned block of 128 rows (0 to 127, 128 to 255, ...) at most 96 rows name the same one
- encoder_weight: bfloat16 [8192, 1024], P(('groups', 'row'), 'lat'), parts along dimension 0, may hold values from -0.09375 to 0.09375
- encoder_bias: float32 [2048], P(('groups', 'lat')), parts along dimension 0, may hold values from -3 to 3
- decoder_weight: bfloat16 [2048, 4096], P(('groups', 'lat'), 'row'), parts along dimension 0, may hold values from -0.3125 to 0.3125
- decoder_bias: float32 [8192], P(('groups', 'row')), parts along dimension 0, may hold values from -3 to 3
- encoder_first: bfloat16 [8192, 1024], P(('groups', 'row'), 'lat'), parts along dimension 0, may hold values from -2 to 2
- encoder_second: bfloat16 [8192, 1024], P(('groups', 'row'), 'lat'), parts along dimension 0, may hold values from 0.0099487305 to 1
- decoder_first: bfloat16 [2048, 4096], P(('groups', 'lat'), 'row'), parts along dimension 0, may hold values from -2 to 2
- decoder_second: bfloat16 [2048, 4096], P(('groups', 'lat'), 'row'), parts along dimension 0, may hold values from 0.0099487305 to 1
Outputs:
- encoder_next: bfloat16 [8192, 1024], P(('groups', 'row'), 'lat'), parts along dimension 0
- encoder_first_next: bfloat16 [8192, 1024], P(('groups', 'row'), 'lat'), parts along dimension 0
- encoder_second_next: bfloat16 [8192, 1024], P(('groups', 'row'), 'lat'), parts along dimension 0
- decoder_next: bfloat16 [2048, 4096], P(('groups', 'lat'), 'row'), parts along dimension 0
- decoder_first_next: bfloat16 [2048, 4096], P(('groups', 'lat'), 'row'), parts along dimension 0
- decoder_second_next: bfloat16 [2048, 4096], P(('groups', 'lat'), 'row'), parts along dimension 0
- encoder_bias_grad: float32 [2048], P(('groups', 'lat')), parts along dimension 0
- decoder_bias_grad: float32 [8192], P(('groups', 'row')), parts along dimension 0
There are 2 independent parts, one for each index of `groups`. A program takes and returns all parts, laid end to end along the dimension named above; each array names one. Nothing has to cross between parts.
Inputs may be any that keep to these rules, and one draw needn't show every extreme that they name: `active_blocks`: each row names 3 different latent blocks. In every aligned block of 128 rows (the rows of one index of lat) no latent block is named by more than 96 rows, and some latent block is named by exactly 96 of them. Every latent block is named by some row.
All inputs are finite; a program needn't handle non-finite values.
Results may differ from a plain program's by a relative error of at most 0.0056.
Values may be sent and summed in bfloat16 or wider, within the bound.
A program may use at most 64 MiB of HBM per device.

v0:
```python
import math

import jax
import jax.numpy as jnp
from jax import lax
from jax.sharding import PartitionSpec as P

beta_one = 0.9
beta_two = 0.999
step_rate = 0.01
epsilon = 1e-08


def adam_update(weight, moment_one, moment_two, gradient):
    first_next = beta_one * moment_one.astype(jnp.float32) + (1.0 - beta_one) * gradient
    second_next = beta_two * moment_two.astype(jnp.float32) + (1.0 - beta_two) * gradient * gradient
    weight_next = weight.astype(jnp.float32) - step_rate * first_next / (
        jnp.sqrt(second_next) + epsilon
    )
    return (
        weight_next.astype(jnp.bfloat16),
        first_next.astype(jnp.bfloat16),
        second_next.astype(jnp.bfloat16),
    )


def contract_rows(left, right):
    return lax.dot_general(
        left, right, (((0,), (0,)), ((), ())), preferred_element_type=jnp.float32
    )


def contract_cols(left, right):
    return lax.dot_general(
        left, right, (((1,), (1,)), ((), ())), preferred_element_type=jnp.float32
    )


def on_device(
    stream_rows,
    active_blocks,
    encoder_weight,
    encoder_bias,
    decoder_weight,
    decoder_bias,
    encoder_first,
    encoder_second,
    decoder_first,
    decoder_second,
):
    lat_count = lax.axis_size("lat")
    row_count = stream_rows.shape[0]
    width_part = stream_rows.shape[1]
    picks = active_blocks.shape[1]
    capacity = min(row_count, 2 * row_count * picks // lat_count)
    slot_total = lat_count * capacity
    loss_scale = 1.0 / math.sqrt(picks * row_count)
    chosen = active_blocks.reshape(-1)
    one_hot = (chosen[:, None] == jnp.arange(lat_count, dtype=jnp.int32)[None, :]).astype(jnp.int32)
    position = jnp.sum((jnp.cumsum(one_hot, axis=0) - 1) * one_hot, axis=1)
    slot_index = chosen * capacity + position
    owner_row = jnp.arange(chosen.shape[0], dtype=jnp.int32) // picks
    slot_row = jnp.zeros((slot_total,), jnp.int32).at[slot_index].set(owner_row)
    slot_live = jnp.zeros((slot_total,), jnp.bfloat16).at[slot_index].set(1.0)
    outgoing = (stream_rows[slot_row] * slot_live[:, None]).reshape(lat_count, capacity, width_part)
    routed_rows = lax.all_to_all(outgoing, "lat", split_axis=0, concat_axis=0, tiled=True).reshape(
        slot_total, width_part
    )
    preact_part = jnp.dot(routed_rows, encoder_weight, preferred_element_type=jnp.float32)
    preact = lax.psum(preact_part, "row") + encoder_bias
    code_vals = jax.nn.softplus(preact).astype(jnp.bfloat16)
    portion = jnp.dot(code_vals, decoder_weight, preferred_element_type=jnp.float32).astype(
        jnp.bfloat16
    )
    returned = lax.all_to_all(
        portion.reshape(lat_count, capacity, width_part),
        "lat",
        split_axis=0,
        concat_axis=0,
        tiled=True,
    )
    picked = returned.reshape(slot_total, width_part)[slot_index].reshape(
        row_count, picks, width_part
    )
    rebuilt = jnp.sum(picked.astype(jnp.float32), axis=1) + decoder_bias
    residual = rebuilt - stream_rows.astype(jnp.float32)
    decoder_bias_grad = lax.psum(loss_scale * jnp.sum(residual, axis=0), "lat")
    error_local = (residual * loss_scale).astype(jnp.bfloat16)
    outgoing_error = (error_local[slot_row] * slot_live[:, None]).reshape(
        lat_count, capacity, width_part
    )
    routed_error = lax.all_to_all(
        outgoing_error, "lat", split_axis=0, concat_axis=0, tiled=True
    ).reshape(slot_total, width_part)
    code_part = contract_cols(routed_error, decoder_weight)
    code_grad = lax.psum(code_part, "row")
    preact_grad = code_grad * jax.nn.sigmoid(preact)
    encoder_bias_grad = jnp.sum(preact_grad, axis=0)
    preact_low = preact_grad.astype(jnp.bfloat16)
    encoder_grad = contract_rows(routed_rows, preact_low)
    decoder_grad = contract_rows(code_vals, routed_error)
    encoder_next, encoder_first_next, encoder_second_next = adam_update(
        encoder_weight, encoder_first, encoder_second, encoder_grad
    )
    decoder_next, decoder_first_next, decoder_second_next = adam_update(
        decoder_weight, decoder_first, decoder_second, decoder_grad
    )
    return (
        encoder_next,
        encoder_first_next,
        encoder_second_next,
        decoder_next,
        decoder_first_next,
        decoder_second_next,
        encoder_bias_grad,
        decoder_bias_grad,
    )


def solution(mesh):
    return jax.shard_map(
        on_device,
        mesh=mesh,
        in_specs=(
            P(("groups", "lat"), "row"),
            P(("groups", "lat"), None),
            P(("groups", "row"), "lat"),
            P(("groups", "lat")),
            P(("groups", "lat"), "row"),
            P(("groups", "row")),
            P(("groups", "row"), "lat"),
            P(("groups", "row"), "lat"),
            P(("groups", "lat"), "row"),
            P(("groups", "lat"), "row"),
        ),
        out_specs=(
            P(("groups", "row"), "lat"),
            P(("groups", "row"), "lat"),
            P(("groups", "row"), "lat"),
            P(("groups", "lat"), "row"),
            P(("groups", "lat"), "row"),
            P(("groups", "lat"), "row"),
            P(("groups", "lat")),
            P(("groups", "row")),
        ),
        check_vma=False,
    )
```

profile of v0, /device:TPU:1, one launch (start us, length us, event | category | flops | bytes accessed | tf_op | source)
XLA Modules:
  0.0 353.4 jit_solution(5224115903619733300)
XLA Ops:
  7.2 0.8 copy.19
  9.1 0.9 reduce-window.6
  10.7 2.9 scatter_custom_fusion
  13.7 3.0 scatter_custom_fusion.1
  16.7 7.4 %gather_fusion = bf16[768,2048]{1,0:T(8,128)(2,1)S(1)} fusion(bf16[128,2048]{1,0:T(8,128)(2,1)} %param.10, s32[1024]{0:T(1024)S(1)} %pad_clamp_fusion.1), kind=kCustom, calls=%fused_computation | custom fusion | bytes 6294528 | tf_op jit(solution)/shard_map/gather | solution.py:65
  24.5 76.8 %all_to_all.15 = bf16[8,96,2048]{2,1,0:T(8,128)(2,1)S(1)} all-to-all(bf16[8,96,2048]{2,1,0:T(8,128)(2,1)S(1)} %broadcast_multiply_fusion.1), channel_id=1, replica_groups=mesh['groups'=2,'lat'=8,'row'=2] {'lat'}, dimensions={0} | all-to-all | bytes 6291456 | tf_op jit(solution)/shard_map/all_to_all | solution.py:66
  101.3 1.7 copy-done.1
  102.9 1.7 fusion.24
  104.7 25.2 %all-reduce.3.cloned.1.call-done = f32[768,128]{1,0:T(8,128)} async-done(((f32[768,128]{1,0:T(8,128)}), f32[768,128]{1,0:T(8,128)}) %all-reduce.3.cloned.1.call-update) | async-done | bytes 393232 | tf_op jit(solution)/shard_map/psum | solution.py:70
  129.8 3.7 %convolution_convert_fusion = bf16[768,2048]{1,0:T(8,128)(2,1)} fusion(bf16[128,2048]{1,0:T(8,128)(2,1)S(1)} %copy-done.4, f32[768,128]{1,0:T(8,128)} %all-reduce.3.cloned.1.call-done, f32[128]{0:T(128)S(1)} %copy-done.8), kind=kOutput, calls=%fused_computation.5 | convolution fusion | flops 405012480 | bytes 4063744 | tf_op jit(solution)/shard_map/dot_general | solution.py:72
  133.5 5.3 %all-to-all-start.1 = ((bf16[8,96,2048]{2,1,0:T(8,128)(2,1)}), bf16[8,96,2048]{2,1,0:T(8,128)(2,1)S(1)}, u32[]{:S(2)}, u32[]{:S(2)}) async-start(bf16[8,96,2048]{2,1,0:T(8,128)(2,1)} %bitcast.25), calls=%async_computation.1 | async-start | bytes 6291456 | tf_op jit(solution)/shard_map/all_to_all | solution.py:75
  138.8 70.7 %all-to-all-done.1 = bf16[8,96,2048]{2,1,0:T(8,128)(2,1)S(1)} async-done(((bf16[8,96,2048]{2,1,0:T(8,128)(2,1)}), bf16[8,96,2048]{2,1,0:T(8,128)(2,1)S(1)}, u32[]{:S(2)}, u32[]{:S(2)}) %all-to-all-start.1) | async-done | bytes 3145760 | tf_op jit(solution)/shard_map/all_to_all | solution.py:75
  209.5 3.2 gather_fusion.1
  212.6 5.5 %reshape.100 = f32[128,3,2048]{2,1,0:T(4,128)} reshape(bf16[384,2048]{1,0:T(8,128)(2,1)} %gather_fusion.1) | data formatting | bytes 4718592 | tf_op jit(solution)/shard_map/convert_element_type | solution.py:85
  218.1 4.9 %reduce_sum.40 = f32[128,2048]{1,0:T(8,128)S(1)} reduce(f32[128,3,2048]{2,1,0:T(4,128)} %reshape.100, f32[]{:T(128)} %constant.28.clone.1), dimensions={1}, to_apply=%region_6.7 | reduce | flops 524288 | bytes 4194308 | tf_op jit(solution)/shard_map/reduce_sum | solution.py:85
  223.2 4.2 %gather_fusion.2 = bf16[768,2048]{1,0:T(8,128)(2,1)} fusion(bf16[128,2048]{1,0:T(8,128)(2,1)S(1)} %get-tuple-element.9, s32[1024]{0:T(1024)S(1)} %pad_clamp_fusion.1), kind=kCustom, calls=%fused_computation.2 | custom fusion | bytes 6294528 | tf_op jit(solution)/shard_map/gather | solution.py:89
  227.5 3.9 %broadcast_multiply_fusion = bf16[8,96,2048]{2,1,0:T(8,128)(2,1)} fusion(bf16[8,96,2048]{2,1,0:T(8,128)(2,1)} %bitcast.26, bf16[8,96]{1,0:T(8,128)(2,1)S(1)} %mul.124), kind=kLoop, calls=%fused_computation.8 | loop fusion | flops 1572864 | bytes 6292992 | tf_op jit(solution)/shard_map/mul | solution.py:89
  231.4 4.4 %all-to-all-start.2 = ((bf16[8,96,2048]{2,1,0:T(8,128)(2,1)}), bf16[8,96,2048]{2,1,0:T(8,128)(2,1)S(1)}, u32[]{:S(2)}, u32[]{:S(2)}) async-start(bf16[8,96,2048]{2,1,0:T(8,128)(2,1)} %broadcast_multiply_fusion), calls=%async_computation.2 | async-start | bytes 6291456 | tf_op jit(solution)/shard_map/all_to_all | solution.py:92
  235.8 75.4 %psum.23 = f32[2048]{0:T(1024)} all-reduce(f32[2048]{0:T(1024)S(1)} %broadcast_multiply_fusion.2), channel_id=1, replica_groups=mesh['groups'=2,'lat'=8,'row'=2] {'lat'}, use_global_device_ids=true, to_apply=%region_10.11 | all-reduce | flops 2048 | bytes 16384 | tf_op jit(solution)/shard_map/psum | solution.py:87
  311.2 3.1 fusion.25
  314.4 5.1 %fusion.5 = (bf16[128,2048]{1,0:T(8,128)(2,1)}, bf16[128,2048]{1,0:T(8,128)(2,1)}, bf16[128,2048]{1,0:T(8,128)(2,1)}) fusion(bf16[128,2048]{1,0:T(8,128)(2,1)} %param.19, bf16[128,2048]{1,0:T(8,128)(2,1)} %param.18, bf16[128,2048]{1,0:T(8,128)(2,1)} %param.14, bf16[768,2048]{1,0:T(8,128)(2,1)} %bitcast.24, f32[768,128]{1,0:T(8,128)S(1)} %copy-done.5, ...), kind=kOutput, calls=%fused_computation.22 | convolution fusion | flops 407896064 | bytes 6685184 | tf_op jit(solution)/shard_map/dot_general | solution.py:28
  319.5 21.2 %all-reduce.5.cloned.1.call-done = f32[768,128]{1,0:T(8,128)} async-done(((f32[768,128]{1,0:T(8,128)}), f32[768,128]{1,0:T(8,128)}) %all-reduce.5.cloned.1.call-update) | async-done | bytes 393232 | tf_op jit(solution)/shard_map/psum | solution.py:96
  340.7 1.6 fusion.23
  342.3 4.3 %fusion.6 = (bf16[2048,128]{1,0:T(8,128)(2,1)}, bf16[2048,128]{1,0:T(8,128)(2,1)}, bf16[2048,128]{1,0:T(8,128)(2,1)}) fusion(bf16[2048,128]{1,0:T(8,128)(2,1)} %param.17, bf16[2048,128]{1,0:T(8,128)(2,1)} %param.16, bf16[2048,128]{1,0:T(8,128)(2,1)} %param.12, bf16[768,2048]{1,0:T(8,128)(2,1)S(1)} %bitcast.22, f32[768,128]{1,0:T(8,128)} %all-reduce.5.cloned.1.call-done, ...), kind=kOutput, calls=%fused_computation.23 | convolution fusion | flops 407699456 | bytes 7078400 | tf_op jit(solution)/shard_map/dot_general | solution.py:28
  (43 shorter events, 2.5 us)
Async XLA Ops:
  7.2 122.7 %all-reduce.3.cloned.1.call-start = ((), (), s32[]{:S(2)}) async-start(), calls=%async_computation.3 | async-start | bytes 786432 | tf_op jit(solution)/shard_map/psum | solution.py:70
  24.4 78.5 %copy-start.6 = (bf16[2048,128]{1,0:T(8,128)(2,1)S(1)}, bf16[2048,128]{1,0:T(8,128)(2,1)}, u32[]{:S(2)}) copy-start(bf16[2048,128]{1,0:T(8,128)(2,1)} %param.12) | copy-start | bytes 1572868
  101.3 1.7 copy-start.1
  101.3 28.6 %copy-start.4 = (bf16[128,2048]{1,0:T(8,128)(2,1)S(1)}, bf16[128,2048]{1,0:T(8,128)(2,1)}, u32[]{:S(2)}) copy-start(bf16[128,2048]{1,0:T(8,128)(2,1)} %param.14) | copy-start | bytes 1572868
  101.3 28.6 %copy-start.8 = (f32[128]{0:T(128)S(1)}, f32[128]{0:T(128)}, u32[]{:S(2)}) copy-start(f32[128]{0:T(128)} %param.13) | copy-start | bytes 1540
  133.5 75.9 %all-to-all-start.1 = ((bf16[8,96,2048]{2,1,0:T(8,128)(2,1)}), bf16[8,96,2048]{2,1,0:T(8,128)(2,1)S(1)}, u32[]{:S(2)}, u32[]{:S(2)}) async-start(bf16[8,96,2048]{2,1,0:T(8,128)(2,1)} %bitcast.25), calls=%async_computation.1 | async-start | bytes 6291456 | tf_op jit(solution)/shard_map/all_to_all | solution.py:75
  218.1 4.9 %copy-start = (bf16[128,2048]{1,0:T(8,128)(2,1)S(1)}, bf16[128,2048]{1,0:T(8,128)(2,1)}, u32[]{:S(2)}) copy-start(bf16[128,2048]{1,0:T(8,128)(2,1)} %param.10) | copy-start | bytes 1572868
  218.1 4.9 %copy-start.7 = (f32[2048]{0:T(1024)S(1)}, f32[2048]{0:T(1024)}, u32[]{:S(2)}) copy-start(f32[2048]{0:T(1024)} %param.15) | copy-start | bytes 24580
  231.4 79.9 %all-to-all-start.2 = ((bf16[8,96,2048]{2,1,0:T(8,128)(2,1)}), bf16[8,96,2048]{2,1,0:T(8,128)(2,1)S(1)}, u32[]{:S(2)}, u32[]{:S(2)}) async-start(bf16[8,96,2048]{2,1,0:T(8,128)(2,1)} %broadcast_multiply_fusion), calls=%async_computation.2 | async-start | bytes 6291456 | tf_op jit(solution)/shard_map/all_to_all | solution.py:92
  235.8 78.6 %copy-start.5 = (f32[768,128]{1,0:T(8,128)S(1)}, f32[768,128]{1,0:T(8,128)}, u32[]{:S(2)}) copy-start(f32[768,128]{1,0:T(8,128)} %all-reduce.3.cloned.1.call-done) | copy-start | bytes 1179652
  235.8 104.9 %all-reduce.5.cloned.1.call-start = ((), (), s32[]{:S(2)}) async-start(), calls=%async_computation.4 | async-start | bytes 786432 | tf_op jit(solution)/shard_map/psum | solution.py:96
  311.2 3.1 copy-start.3
  314.4 26.3 %copy-start.9 = (f32[128]{0:T(128)S(1)}, f32[128]{0:T(128)}, u32[]{:S(2)}) copy-start(f32[128]{0:T(128)} %param.13) | copy-start | bytes 1540
  314.4 27.9 %copy-start.2 = (bf16[8,96,2048]{2,1,0:T(8,128)(2,1)S(1)}, bf16[8,96,2048]{2,1,0:T(8,128)(2,1)}, u32[]{:S(2)}) copy-start(bf16[8,96,2048]{2,1,0:T(8,128)(2,1)} %copy-done.1) | copy-start | bytes 9437188
Sparse Core Ops, SparseCore 0:
  104.8 24.9 all-reduce.2
  314.5 26.1 all-reduce.4
where the time goes:
time: 355 us; the launch traced here: 353 us
  blocking collectives  152 us (43%)
  waiting for transfers between devices  117 us (33%)
  local copies, waits for them, and re-layouts  29.7 us (8%)
  matrix products  17.9 us (5%)
  between operations  14.2 us (4%)
  other arithmetic  12.6 us (4%)
  starting transfers between devices  9.74 us (3%)
    all_to_all x1, blocking collectives, on_device(): lax.all_to_all(outgoing, 'lat', split_axis=0, concat_axis=0, tiled=True)  76.8 us
    psum x1, blocking collectives, on_device(): decoder_bias_grad = lax.psum(loss_scale * jnp.sum(residual, axis=0), 'lat')  75.4 us
    all_to_all x1, waiting for transfers between devices, on_device(): lax.all_to_all(portion.reshape(lat_count, capacity, width_part), 'lat', s...  70.7 us
    psum x1, waiting for transfers between devices, on_device(): preact = lax.psum(preact_part, 'row') + encoder_bias  25.2 us
    psum x1, waiting for transfers between devices, on_device(): code_grad = lax.psum(code_part, 'row')  21.2 us
    dot_general x2, matrix products, contract_rows(): lax.dot_general(left, right, (((0,), (0,)), ((), ())), preferred_element_...  9.33 us
    gather x1, local copies, waits for them, and re-layouts, on_device(): stream_rows[slot_row] * slot_live[:, None]  7.45 us
  transfers between devices with their start and end apart: 4, of which 3 were waited for; matrix products, arithmetic and copies ran while one was open for 1% of the time, Pallas kernels for 0%

commit v1 on v0

--- a/solution.py
+++ b/solution.py
@@ -36,7 +36,7 @@
     )
 
 
-def on_device(
+def routed_step(
     stream_rows,
     active_blocks,
     encoder_weight,
@@ -117,9 +117,77 @@
     )
 
 
+def gathered_step(
+    stream_rows,
+    active_blocks,
+    encoder_weight,
+    encoder_bias,
+    decoder_weight,
+    decoder_bias,
+    encoder_first,
+    encoder_second,
+    decoder_first,
+    decoder_second,
+):
+    lat_count = lax.axis_size("lat")
+    lat_here = lax.axis_index("lat")
+    row_count, width_part = stream_rows.shape
+    picks = active_blocks.shape[1]
+    block = encoder_weight.shape[1]
+    loss_scale = 1.0 / math.sqrt(picks * row_count)
+    rows_all = lax.all_gather(stream_rows, "lat", axis=0, tiled=True)
+    decoder_all = lax.all_gather(decoder_weight, "lat", axis=0, tiled=True)
+    blocks_all = lax.all_gather(active_blocks, "lat", axis=0, tiled=True)
+    live = jnp.any(blocks_all == lat_here, axis=1)[:, None]
+    preact_part = jnp.dot(rows_all, encoder_weight, preferred_element_type=jnp.float32)
+    preact = lax.psum(preact_part, "row") + encoder_bias
+    code_vals = jnp.where(live, jax.nn.softplus(preact), 0.0).astype(jnp.bfloat16)
+    codes_here = lax.all_to_all(
+        code_vals.reshape(lat_count, row_count, block), "lat", split_axis=0, concat_axis=0, tiled=True
+    )
+    codes_here = codes_here.transpose(1, 0, 2).reshape(row_count, lat_count * block)
+    rebuilt = (
+        jnp.dot(codes_here, decoder_all, preferred_element_type=jnp.float32) + decoder_bias
+    )
+    residual = rebuilt - stream_rows.astype(jnp.float32)
+    decoder_bias_grad = lax.psum(loss_scale * jnp.sum(residual, axis=0), "lat")
+    error_local = (residual * loss_scale).astype(jnp.bfloat16)
+    errors_all = lax.all_gather(error_local, "lat", axis=0, tiled=True)
+    code_part = contract_cols(error_local, decoder_all)
+    code_grad = lax.psum(code_part, "row").astype(jnp.bfloat16)
+    code_grad = lax.all_to_all(
+        code_grad.reshape(row_count, lat_count, block).transpose(1, 0, 2),
+        "lat",
+        split_axis=0,
+        concat_axis=0,
+        tiled=True,
+    ).reshape(lat_count * row_count, block)
+    preact_grad = jnp.where(live, code_grad.astype(jnp.float32) * jax.nn.sigmoid(preact), 0.0)
+    encoder_bias_grad = jnp.sum(preact_grad, axis=0)
+    preact_low = preact_grad.astype(jnp.bfloat16)
+    encoder_grad = contract_rows(rows_all, preact_low)
+    decoder_grad = contract_rows(code_vals, errors_all)
+    encoder_next, encoder_first_next, encoder_second_next = adam_update(
+        encoder_weight, encoder_first, encoder_second, encoder_grad
+    )
+    decoder_next, decoder_first_next, decoder_second_next = adam_update(
+        decoder_weight, decoder_first, decoder_second, decoder_grad
+    )
+    return (
+        encoder_next,
+        encoder_first_next,
+        encoder_second_next,
+        decoder_next,
+        decoder_first_next,
+        decoder_second_next,
+        encoder_bias_grad,
+        decoder_bias_grad,
+    )
+
+
 def solution(mesh):
     return jax.shard_map(
-        on_device,
+        gathered_step if mesh.shape["lat"] <= 8 else routed_step,
         mesh=mesh,
         in_specs=(
             P(("groups", "lat"), "row"),

time: 355 us -> 217 us (0.61)
  blocking collectives: 152 us -> 49.1 us
  local copies, waits for them, and re-layouts: 29.7 us -> 7.11 us
  other arithmetic: 12.6 us -> 2.16 us
  waiting for transfers between devices: 117 us -> 111 us
  matrix products: 17.9 us -> 21.7 us
    all_gather x0 -> x3, waiting for transfers between devices: none -> 96.5 us  [the longest x1 51.3 us: gathered_step(): rows_all = lax.all_gather(stream_rows, 'lat', axis=0, tiled=True)]
    all_to_all x1 -> x0, blocking collectives: 76.8 us -> none  [on_device(): lax.all_to_all(outgoing, 'lat', split_axis=0, concat_axis=0, tiled=True)]
    all_to_all x2, waiting for transfers between devices: 70.7 us -> 0.01 us  [the longest x1 0.01 us: gathered_step(): lax.all_to_all(code_grad.reshape(row_count, lat_count, block).transpose(1...]
    psum x1 -> x2, blocking collectives: 75.4 us -> 36.3 us  [the longest x1 20.3 us: gathered_step(): decoder_bias_grad = lax.psum(loss_scale * jnp.sum(residual, axis=0), 'lat')]
    psum x2 -> x1, waiting for transfers between devices: 46.3 us -> 13.5 us  [gathered_step(): preact = lax.psum(preact_part, 'row') + encoder_bias]
    gather x3 -> x0, local copies, waits for them, and re-layouts: 14.8 us -> none  [the longest x1 7.45 us: on_device(): stream_rows[slot_row] * slot_live[:, None]]
    all_gather x0 -> x1, blocking collectives: none -> 12.8 us  [gathered_step(): blocks_all = lax.all_gather(active_blocks, 'lat', axis=0, tiled=True)]
    reduce_sum x4 -> x1, other arithmetic: 6.83 us -> 0.74 us  [gathered_step(): encoder_bias_grad = jnp.sum(preact_grad, axis=0)]
  transfers between devices with their start and end apart: 4 -> 6, of which waited for: 3 -> 3; matrix products, arithmetic and copies ran while one was open for 1% -> 8% of each run, Pallas kernels for 0% -> 0%
where the time goes in v1:
time: 217 us; the launch traced here: 216 us
  waiting for transfers between devices  111 us (51%)
  blocking collectives  49.1 us (23%)
  matrix products  21.7 us (10%)
  between operations  13.9 us (6%)
  starting transfers between devices  10.2 us (5%)
  local copies, waits for them, and re-layouts  7.11 us (3%)
    all_gather x1, waiting for transfers between devices, gathered_step(): rows_all = lax.all_gather(stream_rows, 'lat', axis=0, tiled=True)  51.3 us
    all_gather x1, waiting for transfers between devices, gathered_step(): decoder_all = lax.all_gather(decoder_weight, 'lat', axis=0, tiled=True)  45.2 us
    psum x1, blocking collectives, gathered_step(): decoder_bias_grad = lax.psum(loss_scale * jnp.sum(residual, axis=0), 'lat')  20.3 us
    psum x1, blocking collectives, gathered_step(): code_grad = lax.psum(code_part, 'row').astype(jnp.bfloat16)  16 us
    psum x1, waiting for transfers between devices, gathered_step(): preact = lax.psum(preact_part, 'row') + encoder_bias  13.5 us
    all_gather x1, blocking collectives, gathered_step(): blocks_all = lax.all_gather(active_blocks, 'lat', axis=0, tiled=True)  12.8 us
    dot_general x2, matrix products, contract_rows(): lax.dot_general(left, right, (((0,), (0,)), ((), ())), preferred_element_...  9.6 us
    unnamed x24, local copies, waits for them, and re-layouts  5.51 us
  transfers between devices with their start and end apart: 6, of which 3 were waited for; matrix products, arithmetic and copies ran while one was open for 8% of the time, Pallas kernels for 0%

profile of v1, /device:TPU:1, one launch (start us, length us, event | category | flops | bytes accessed | tf_op | source)
XLA Modules:
  0.0 215.5 jit_solution(13190653157884613985)
XLA Ops:
  7.2 0.7 all-gather.4.cloned.1.call-update
  8.0 51.3 %all-gather.4.cloned.1.call-done = bf16[1024,2048]{1,0:T(8,128)(2,1)} async-done(((bf16[128,2048]{1,0:T(8,128)(2,1)}), bf16[1024,2048]{1,0:T(8,128)(2,1)}) %all-gather.4.cloned.1.call-update) | async-done | bytes 4194320 | tf_op jit(solution)/shard_map/all_gather | solution.py:138
  59.3 4.3 %fusion.14 = f32[1024,128]{1,0:T(8,128)} fusion(bf16[1024,2048]{1,0:T(8,128)(2,1)} %all-gather.4.cloned.1.call-done, bf16[2048,128]{1,0:T(8,128)(2,1)} %param.12), kind=kOutput, calls=%fused_computation.28 | convolution fusion | flops 536870912 | bytes 5242880 | tf_op jit(solution)/shard_map/dot_general | solution.py:142
  63.7 0.7 all-gather.6.cloned.1.call-update
  64.4 12.8 %all_gather.12 = s32[1024,3]{0,1:T(4,128)S(1)} all-gather(s32[128,3]{0,1:T(4,128)S(1)} %copy-done.7), channel_id=1, replica_groups=mesh['groups'=2,'lat'=8,'row'=2] {'lat'}, dimensions={0}, use_global_device_ids=true | all-gather | bytes 13824 | tf_op jit(solution)/shard_map/all_gather | solution.py:140
  77.2 13.5 %all-reduce.3.cloned.1.call-done = f32[1024,128]{1,0:T(8,128)} async-done(((f32[1024,128]{1,0:T(8,128)}), f32[1024,128]{1,0:T(8,128)}) %all-reduce.3.cloned.1.call-update) | async-done | bytes 524304 | tf_op jit(solution)/shard_map/psum | solution.py:143
  90.7 1.4 fusion.8
  92.1 0.9 copy.27
  93.0 5.3 %all-to-all-start = ((bf16[8,128,128]{1,2,0:T(8,128)(2,1)}), bf16[8,128,128]{1,2,0:T(8,128)(2,1)S(1)}, u32[]{:S(2)}, u32[]{:S(2)}) async-start(bf16[8,128,128]{1,2,0:T(8,128)(2,1)} %copy.27), calls=%async_computation | async-start | bytes 524288 | tf_op jit(solution)/shard_map/all_to_all | solution.py:145
  98.2 45.2 %all-gather.6.cloned.1.call-done = bf16[1024,2048]{1,0:T(8,128)(2,1)} async-done(((bf16[128,2048]{1,0:T(8,128)(2,1)}), bf16[1024,2048]{1,0:T(8,128)(2,1)}) %all-gather.6.cloned.1.call-update) | async-done | bytes 4194320 | tf_op jit(solution)/shard_map/all_gather | solution.py:139
  143.4 3.8 %fusion.13 = (f32[2048]{0:T(1024)S(1)}, bf16[128,2048]{1,0:T(8,128)(2,1)}) fusion(bf16[128,2048]{1,0:T(8,128)(2,1)S(1)} %copy-done.2, f32[2048]{0:T(1024)S(1)} %copy-done.6, bf16[128,1024]{0,1:T(8,128)(2,1)S(1)} %bitcast.30, bf16[1024,2048]{1,0:T(8,128)(2,1)} %all-gather.6.cloned.1.call-done), kind=kOutput, calls=%fused_computation.27 | convolution fusion | flops 538441728 | bytes 5521408 | tf_op jit(solution)/shard_map/dot_general | solution.py:150
  147.3 4.0 %fusion.15 = f32[128,1024]{1,0:T(8,128)S(1)} fusion(bf16[128,2048]{1,0:T(8,128)(2,1)} %get-tuple-element.33, bf16[1024,2048]{1,0:T(8,128)(2,1)} %all-gather.6.cloned.1.call-done), kind=kOutput, calls=%fused_computation.29 | convolution fusion | flops 536870912 | bytes 5242880 | tf_op jit(solution)/shard_map/dot_general | solution.py:34
  151.3 16.0 %all-reduce.4 = bf16[128,1024]{1,0:T(8,128)(2,1)S(1)} all-reduce(f32[128,1024]{1,0:T(8,128)S(1)} %fusion.15), channel_id=1, replica_groups=mesh['groups'=2,'lat'=8,'row'=2] {'row'}, use_global_device_ids=true, to_apply=%region_2.3 | all-reduce | flops 131072 | bytes 786432 | tf_op jit(solution)/shard_map/psum | solution.py:157
  167.3 0.8 bitcast_bitcast_fusion
  168.0 4.8 %all-to-all-start.1 = ((bf16[8,128,128]{2,1,0:T(8,128)(2,1)}), bf16[8,128,128]{2,1,0:T(8,128)(2,1)S(1)}, u32[]{:S(2)}, u32[]{:S(2)}) async-start(bf16[8,128,128]{2,1,0:T(8,128)(2,1)} %bitcast_bitcast_fusion), calls=%async_computation.1 | async-start | bytes 524288 | tf_op jit(solution)/shard_map/all_to_all | solution.py:158
  172.8 0.2 copy.25
  173.0 1.0 copy.26
  174.3 20.3 %psum.23 = f32[2048]{0:T(1024)} all-reduce(f32[2048]{0:T(1024)S(1)} %broadcast_multiply_fusion), channel_id=1, replica_groups=mesh['groups'=2,'lat'=8,'row'=2] {'lat'}, use_global_device_ids=true, to_apply=%region_5.6 | all-reduce | flops 2048 | bytes 16384 | tf_op jit(solution)/shard_map/psum | solution.py:153
  194.6 0.7 fusion.11
  195.4 4.6 %fusion.6 = (bf16[2048,128]{0,1:T(8,128)(2,1)S(1)}, bf16[2048,128]{0,1:T(8,128)(2,1)}, bf16[2048,128]{0,1:T(8,128)(2,1)S(1)}) fusion(bf16[2048,128]{0,1:T(8,128)(2,1)S(1)} %copy.29, bf16[2048,128]{0,1:T(8,128)(2,1)} %copy.26, bf16[2048,128]{0,1:T(8,128)(2,1)S(1)} %copy.25, bf16[1024,2048]{1,0:T(8,128)(2,1)} %all-gather.4.cloned.1.call-done, ...), kind=kOutput, calls=%fused_computation.16 | convolution fusion | flops 541327360 | bytes 7602176 | tf_op jit(solution)/shard_map/dot_general | solution.py:28
  200.0 2.0 copy.30
  202.0 1.0 copy.31
  203.0 1.0 copy.32
  204.0 5.0 %fusion.5 = (bf16[128,2048]{1,0:T(8,128)(2,1)}, bf16[128,2048]{1,0:T(8,128)(2,1)}, bf16[128,2048]{1,0:T(8,128)(2,1)}) fusion(bf16[128,2048]{1,0:T(8,128)(2,1)} %param.19, bf16[128,2048]{1,0:T(8,128)(2,1)} %param.18, bf16[128,2048]{1,0:T(8,128)(2,1)S(1)} %copy-done.5, bf16[1024,128]{1,0:T(8,128)(2,1)S(1)} %fusion.8, ...), kind=kOutput, calls=%fused_computation.15 | convolution fusion | flops 541327360 | bytes 7602176 | tf_op jit(solution)/shard_map/dot_general | solution.py:28
  (30 shorter events, 0.4 us)
Async XLA Ops:
  7.2 57.2 %copy-start.7 = (s32[128,3]{0,1:T(4,128)S(1)}, s32[128,3]{0,1:T(4,128)}, u32[]{:S(2)}) copy-start(s32[128,3]{0,1:T(4,128)} %param.11) | copy-start | bytes 4612
  7.2 83.5 %copy-start.8 = (f32[128]{0:T(128)S(1)}, f32[128]{0:T(128)}, u32[]{:S(2)}) copy-start(f32[128]{0:T(128)} %param.13) | copy-start | bytes 1540
  7.2 52.1 %all-gather.4.cloned.1.call-start = ((), (), s32[]{:S(2)}) async-start(), calls=%async_computation.2 | async-start | bytes 4718592 | tf_op jit(solution)/shard_map/all_gather | solution.py:138
  7.9 135.5 %copy-start.2 = (bf16[128,2048]{1,0:T(8,128)(2,1)S(1)}, bf16[128,2048]{1,0:T(8,128)(2,1)}, u32[]{:S(2)}) copy-start(bf16[128,2048]{1,0:T(8,128)(2,1)} %param.10) | copy-start | bytes 1572868
  7.9 135.5 %copy-start.6 = (f32[2048]{0:T(1024)S(1)}, f32[2048]{0:T(1024)}, u32[]{:S(2)}) copy-start(f32[2048]{0:T(1024)} %param.15) | copy-start | bytes 24580
  7.9 82.8 %all-reduce.3.cloned.1.call-start = ((), (), s32[]{:S(2)}) async-start(), calls=%async_computation.3 | async-start | bytes 1048576 | tf_op jit(solution)/shard_map/psum | solution.py:143
  63.7 79.8 %all-gather.6.cloned.1.call-start = ((), (), s32[]{:S(2)}) async-start(), calls=%async_computation.4 | async-start | bytes 4718592 | tf_op jit(solution)/shard_map/all_gather | solution.py:139
  93.0 50.4 %all-to-all-start = ((bf16[8,128,128]{1,2,0:T(8,128)(2,1)}), bf16[8,128,128]{1,2,0:T(8,128)(2,1)S(1)}, u32[]{:S(2)}, u32[]{:S(2)}) async-start(bf16[8,128,128]{1,2,0:T(8,128)(2,1)} %copy.27), calls=%async_computation | async-start | bytes 524288 | tf_op jit(solution)/shard_map/all_to_all | solution.py:145
  98.2 105.8 %all-gather.8.cloned.1.call-start = ((), (), s32[]{:S(2)}) async-start(), calls=%async_computation.5 | async-start | bytes 4718592 | tf_op jit(solution)/shard_map/all_gather | solution.py:155
  147.2 25.6 %copy-start = (bf16[2048,128]{1,0:T(8,128)(2,1)S(1)}, bf16[2048,128]{1,0:T(8,128)(2,1)}, u32[]{:S(2)}) copy-start(bf16[2048,128]{1,0:T(8,128)(2,1)} %param.12) | copy-start | bytes 1572868
  147.2 25.8 %copy-start.3 = (bf16[2048,128]{1,0:T(8,128)(2,1)S(1)}, bf16[2048,128]{1,0:T(8,128)(2,1)}, u32[]{:S(2)}) copy-start(bf16[2048,128]{1,0:T(8,128)(2,1)} %param.16) | copy-start | bytes 1572868
  147.2 26.8 %copy-start.4 = (bf16[2048,128]{1,0:T(8,128)(2,1)S(1)}, bf16[2048,128]{1,0:T(8,128)(2,1)}, u32[]{:S(2)}) copy-start(bf16[2048,128]{1,0:T(8,128)(2,1)} %param.17) | copy-start | bytes 1572868
  147.3 47.4 %copy-start.1 = (f32[1024,128]{1,0:T(8,128)S(1)}, f32[1024,128]{1,0:T(8,128)}, u32[]{:S(2)}) copy-start(f32[1024,128]{1,0:T(8,128)} %all-reduce.3.cloned.1.call-done) | copy-start | bytes 1572868
  168.0 26.6 %all-to-all-start.1 = ((bf16[8,128,128]{2,1,0:T(8,128)(2,1)}), bf16[8,128,128]{2,1,0:T(8,128)(2,1)S(1)}, u32[]{:S(2)}, u32[]{:S(2)}) async-start(bf16[8,128,128]{2,1,0:T(8,128)(2,1)} %bitcast_bitcast_fusion), calls=%async_computation.1 | async-start | bytes 524288 | tf_op jit(solution)/shard_map/all_to_all | solution.py:158
  195.4 8.7 %copy-start.5 = (bf16[128,2048]{1,0:T(8,128)(2,1)S(1)}, bf16[128,2048]{1,0:T(8,128)(2,1)}, u32[]{:S(2)}) copy-start(bf16[128,2048]{1,0:T(8,128)(2,1)} %param.14) | copy-start | bytes 1572868
Sparse Core Ops, SparseCore 0:
  9.6 49.6 all-gather.3
  63.8 26.9 all-reduce.2
  92.4 50.9 all-gather.5
  147.4 51.1 all-gather.7

commit v2 on v0

--- a/solution.py
+++ b/solution.py
@@ -1,8 +1,11 @@
+import functools
 import math
 
 import jax
 import jax.numpy as jnp
 from jax import lax
+from jax.experimental import pallas as pl
+from jax.experimental.pallas import tpu as pltpu
 from jax.sharding import PartitionSpec as P
 
 beta_one = 0.9
@@ -36,7 +39,7 @@
     )
 
 
-def on_device(
+def routed_step(
     stream_rows,
     active_blocks,
     encoder_weight,
@@ -117,9 +120,403 @@
     )
 
 
+PIECES = 2
+TILE = 512
+
+
+def step_kernel(
+    lat_count,
+    loss_scale,
+    rows_ref,
+    mask_ref,
+    enc_ref,
+    ebias_ref,
+    dec_ref,
+    dbias_ref,
+    enc_grad_ref,
+    dec_grad_ref,
+    enc_bias_grad_ref,
+    dec_bias_grad_ref,
+    rows_all,
+    dec_all,
+    err_all,
+    masks,
+    part_mine,
+    part_other,
+    preact,
+    code_mine,
+    code_here,
+    grad_mine,
+    grad_other,
+    grad_out,
+    grad_in,
+    sums,
+    gather_send,
+    gather_recv,
+    small_send,
+    small_recv,
+):
+    count, width = rows_ref.shape
+    chips = lat_count // 2
+    me = lax.axis_index("lat")
+    other = 1 - lax.axis_index("row")
+    chip, core = me // 2, me % 2
+    mate = chip * 2 + 1 - core
+    piece = count // PIECES
+    mesh_id = pl.DeviceIdType.MESH
+    buffers = (rows_all, dec_all, err_all)
+
+    barrier = pltpu.get_barrier_semaphore()
+    for step in range(1, lat_count):
+        pl.semaphore_signal(
+            barrier, inc=1, device_id={"lat": (me + step) % lat_count}, device_id_type=mesh_id
+        )
+    pl.semaphore_signal(barrier, inc=1, device_id={"row": other}, device_id_type=mesh_id)
+    pl.semaphore_wait(barrier, lat_count)
+
+    def span(at):
+        return pl.ds(pl.multiple_of(at * count, count), count)
+
+    def gather_copy(which, way, owner, part, target):
+        view = buffers[which].at[pl.ds(pl.multiple_of(owner * count + part * piece, piece), piece)]
+        return pltpu.make_async_remote_copy(
+            src_ref=view,
+            dst_ref=view,
+            send_sem=gather_send.at[which, way, owner, part],
+            recv_sem=gather_recv.at[which, owner, part],
+            device_id={"lat": target},
+            device_id_type=mesh_id,
+        )
+
+    def each_way(which, owner, part, way, act):
+        if way == 0:
+            pl.when(chip < chips - 1)(lambda: act(gather_copy(which, 0, owner, part, me + 2)))
+        elif way == 1:
+            pl.when(chip > 0)(lambda: act(gather_copy(which, 1, owner, part, me - 2)))
+        else:
+            act(gather_copy(which, 2, owner, part, mate))
+
+    def begin(copy):
+        copy.start()
+
+    def sent(copy):
+        copy.wait_send()
+
+    def own_way(which, way):
+        for part in range(PIECES):
+            each_way(which, me, part, way, begin)
+
+    def arrived(which, owner, part):
+        gather_copy(which, 2, owner, part, mate).wait_recv()
+
+    def pass_on(which, step, then=None):
+        for part in range(PIECES):
+            for way, owner, there in (
+                (0, me - 2 * step, chip >= step),
+                (1, me + 2 * step, chip + step < chips),
+            ):
+                @pl.when(there)
+                def _():
+                    arrived(which, owner, part)
+                    each_way(which, owner, part, way, begin)
+                    each_way(which, owner, part, 2, begin)
+                    if then is not None and part == PIECES - 1:
+                        then(owner)
+
+    def from_mate(which, step, then=None):
+        if step == 0:
+            for part in range(PIECES):
+                arrived(which, mate, part)
+            if then is not None:
+                then(mate)
+            return
+        for owner, there in ((mate - 2 * step, chip >= step), (mate + 2 * step, chip + step < chips)):
+            @pl.when(there)
+            def _():
+                for part in range(PIECES):
+                    arrived(which, owner, part)
+                if then is not None:
+                    then(owner)
+
+    def all_sent(which):
+        for part in range(PIECES):
+            for way in range(3):
+                each_way(which, me, part, way, sent)
+        for step in range(1, chips):
+            for part in range(PIECES):
+                for way, owner, there in (
+                    (0, me - 2 * step, chip >= step),
+                    (1, me + 2 * step, chip + step < chips),
+                ):
+                    @pl.when(there)
+                    def _():
+                        each_way(which, owner, part, way, sent)
+                        each_way(which, owner, part, 2, sent)
+
+    def to_lat(kind, source, target_buffer, target):
+        return pltpu.make_async_remote_copy(
+            src_ref=source,
+            dst_ref=target_buffer.at[me],
+            send_sem=small_send.at[kind, target],
+            recv_sem=small_recv.at[kind, me],
+            device_id={"lat": target},
+            device_id_type=mesh_id,
+        )
+
+    def from_lat(kind, target_buffer, source):
+        return pltpu.make_async_remote_copy(
+            src_ref=target_buffer.at[source],
+            dst_ref=target_buffer.at[source],
+            send_sem=small_send.at[kind, source],
+            recv_sem=small_recv.at[kind, source],
+            device_id={"lat": source},
+            device_id_type=mesh_id,
+        )
+
+    def across(kind, mine, theirs, at):
+        return pltpu.make_async_remote_copy(
+            src_ref=mine.at[at],
+            dst_ref=theirs.at[at],
+            send_sem=small_send.at[kind, at],
+            recv_sem=small_recv.at[kind, at],
+            device_id={"row": other},
+            device_id_type=mesh_id,
+        )
+
+    MASK, PART, CODE, GRAD, GRAD_OUT, SUM = range(6)
+
+    rows_all[span(me)] = rows_ref[...]
+    for way in range(3):
+        own_way(0, way)
+    for step in range(1, lat_count):
+        target = (me + step) % lat_count
+        to_lat(MASK, mask_ref.at[target], masks, target).start()
+    masks[me] = mask_ref[me]
+    dec_all[span(me)] = dec_ref[...]
+    own_way(1, 2)
+
+    def encode(owner):
+        part_mine[owner] = jnp.dot(
+            rows_all[span(owner)], enc_ref[...], preferred_element_type=jnp.float32
+        )
+        across(PART, part_mine, part_other, owner).start()
+
+    encode(me)
+    for step in range(chips):
+        if step > 0:
+            pass_on(0, step, encode)
+            from_mate(0, step - 1, encode)
+        pl.when(chip == step)(lambda: own_way(1, 0))
+        pl.when(chip == chips - 1 - step)(lambda: own_way(1, 1))
+    from_mate(0, chips - 1, encode)
+
+    diagonal = lax.broadcasted_iota(jnp.int32, (count, count), 0) == lax.broadcasted_iota(
+        jnp.int32, (count, count), 1
+    )
+
+    def live(owner):
+        row = masks[owner][0:1, :].astype(jnp.float32)
+        return jnp.sum(jnp.where(diagonal, row, 0.0), axis=1, keepdims=True)
+
+    for owner in range(lat_count):
+        @pl.when(owner != me)
+        def _():
+            from_lat(MASK, masks, owner).wait_recv()
+
+        across(PART, part_mine, part_other, owner).wait_recv()
+        value = part_mine[owner] + part_other[owner] + ebias_ref[...]
+        preact[owner] = value
+        soft = jnp.maximum(value, 0.0) + jnp.log1p(jnp.exp(-jnp.abs(value)))
+        code_mine[owner] = (soft * live(owner)).astype(jnp.bfloat16)
+
+        @pl.when(owner != me)
+        def _():
+            to_lat(CODE, code_mine.at[owner], code_here, owner).start()
+
+        @pl.when(owner == me)
+        def _():
+            code_here[owner] = code_mine[owner]
+
+    for step in range(1, chips):
+        pass_on(1, step)
+    for step in range(chips):
+        from_mate(1, step)
+    for owner in range(lat_count):
+        @pl.when(owner != me)
+        def _():
+            from_lat(CODE, code_here, owner).wait_recv()
+
+    codes = jnp.concatenate([code_here[at] for at in range(lat_count)], axis=1)
+    for at in range(0, width, TILE):
+        cols = slice(at, at + TILE)
+        rebuilt = jnp.dot(codes, dec_all[:, cols], preferred_element_type=jnp.float32)
+        residual = rebuilt + dbias_ref[:, cols] - rows_ref[:, cols].astype(jnp.float32)
+        sums[me, :, cols] = loss_scale * jnp.sum(residual, axis=0, keepdims=True)
+        err_all[span(me), cols] = (residual * loss_scale).astype(jnp.bfloat16)
+    for way in range(3):
+        own_way(2, way)
+    errors = err_all[span(me)]
+    for owner in range(lat_count):
+        grad_mine[owner] = lax.dot_general(
+            errors,
+            dec_all[owner * count:(owner + 1) * count],
+            (((1,), (1,)), ((), ())),
+            preferred_element_type=jnp.float32,
+        )
+        across(GRAD, grad_mine, grad_other, owner).start()
+    for step in range(1, lat_count):
+        target = (me + step) % lat_count
+        to_lat(SUM, sums.at[me], sums, target).start()
+    for owner in range(lat_count):
+        across(GRAD, grad_mine, grad_other, owner).wait_recv()
+        grad_out[owner] = (grad_mine[owner] + grad_other[owner]).astype(jnp.bfloat16)
+
+        @pl.when(owner != me)
+        def _():
+            to_lat(GRAD_OUT, grad_out.at[owner], grad_in, owner).start()
+
+        @pl.when(owner == me)
+        def _():
+            grad_in[owner] = grad_out[owner]
+
+    for step in range(1, chips - 1):
+        pass_on(2, step)
+
+    bias_total = jnp.zeros_like(enc_bias_grad_ref)
+    lows = []
+    for owner in range(lat_count):
+        @pl.when(owner != me)
+        def _():
+            from_lat(GRAD_OUT, grad_in, owner).wait_recv()
+
+        grad = grad_in[owner].astype(jnp.float32) * live(owner) * jax.nn.sigmoid(preact[owner])
+        bias_total = bias_total + jnp.sum(grad, axis=0, keepdims=True)
+        lows.append(grad.T.astype(jnp.bfloat16))
+    enc_bias_grad_ref[...] = bias_total
+    lows = jnp.concatenate(lows, axis=1)
+    for at in range(0, width, TILE):
+        cols = slice(at, at + TILE)
+        enc_grad_ref[:, cols] = jnp.dot(lows, rows_all[:, cols], preferred_element_type=jnp.float32)
+    for owner in range(lat_count):
+        @pl.when(owner != me)
+        def _():
+            from_lat(SUM, sums, owner).wait_recv()
+    total = sums[0]
+    for owner in range(1, lat_count):
+        total = total + sums[owner]
+    dec_bias_grad_ref[...] = total
+    turned = jnp.concatenate(
+        [code_mine[at].astype(jnp.float32).T.astype(jnp.bfloat16) for at in range(lat_count)], axis=1
+    )
+
+    if chips > 1:
+        pass_on(2, chips - 1)
+    for step in range(chips):
+        from_mate(2, step)
+    for at in range(0, width, TILE):
+        cols = slice(at, at + TILE)
+        dec_grad_ref[:, cols] = jnp.dot(turned, err_all[:, cols], preferred_element_type=jnp.float32)
+
+    for which in range(3):
+        all_sent(which)
+    for owner in range(lat_count):
+        across(PART, part_mine, part_other, owner).wait_send()
+        across(GRAD, grad_mine, grad_other, owner).wait_send()
+
+        @pl.when(owner != me)
+        def _():
+            to_lat(MASK, mask_ref.at[owner], masks, owner).wait_send()
+            to_lat(CODE, code_mine.at[owner], code_here, owner).wait_send()
+            to_lat(GRAD_OUT, grad_out.at[owner], grad_in, owner).wait_send()
+            to_lat(SUM, sums.at[me], sums, owner).wait_send()
+
+
+def gathered_step(
+    stream_rows,
+    active_blocks,
+    encoder_weight,
+    encoder_bias,
+    decoder_weight,
+    decoder_bias,
+    encoder_first,
+    encoder_second,
+    decoder_first,
+    decoder_second,
+):
+    lat_count = lax.axis_size("lat")
+    row_count, width = stream_rows.shape
+    picks = active_blocks.shape[1]
+    block = encoder_weight.shape[1]
+    loss_scale = 1.0 / math.sqrt(picks * row_count)
+    named = jnp.any(
+        active_blocks[None, :, :] == jnp.arange(lat_count, dtype=jnp.int32)[:, None, None], axis=2
+    )
+    mask = jnp.broadcast_to(named[:, None, :], (lat_count, 16, row_count)).astype(jnp.bfloat16)
+    low, full = jnp.bfloat16, jnp.float32
+    everything = lat_count * row_count
+    blocks = (lat_count, row_count, block)
+    encoder_grad, decoder_grad, encoder_bias_grad, decoder_bias_grad = pl.pallas_call(
+        functools.partial(step_kernel, lat_count, loss_scale),
+        out_shape=(
+            jax.ShapeDtypeStruct((block, width), full),
+            jax.ShapeDtypeStruct((block, width), full),
+            jax.ShapeDtypeStruct((1, block), full),
+            jax.ShapeDtypeStruct((1, width), full),
+        ),
+        in_specs=[pl.BlockSpec(memory_space=pltpu.VMEM)] * 6,
+        out_specs=[pl.BlockSpec(memory_space=pltpu.VMEM)] * 4,
+        scratch_shapes=[
+            pltpu.VMEM((everything, width), low),
+            pltpu.VMEM((everything, width), low),
+            pltpu.VMEM((everything, width), low),
+            pltpu.VMEM((lat_count, 16, row_count), low),
+            pltpu.VMEM(blocks, full),
+            pltpu.VMEM(blocks, full),
+            pltpu.VMEM(blocks, full),
+            pltpu.VMEM(blocks, low),
+            pltpu.VMEM(blocks, low),
+            pltpu.VMEM(blocks, full),
+            pltpu.VMEM(blocks, full),
+            pltpu.VMEM(blocks, low),
+            pltpu.VMEM(blocks, low),
+            pltpu.VMEM((lat_count, 1, width), full),
+            pltpu.SemaphoreType.DMA((3, 3, lat_count, PIECES)),
+            pltpu.SemaphoreType.DMA((3, lat_count, PIECES)),
+            pltpu.SemaphoreType.DMA((6, lat_count)),
+            pltpu.SemaphoreType.DMA((6, lat_count)),
+        ],
+        compiler_params=pltpu.CompilerParams(
+            collective_id=0, has_side_effects=True, vmem_limit_bytes=48 * 1024 * 1024
+        ),
+    )(
+        stream_rows,
+        mask,
+        encoder_weight,
+        encoder_bias.reshape(1, block),
+        decoder_weight,
+        decoder_bias.reshape(1, width),
+    )
+    encoder_next, encoder_first_next, encoder_second_next = adam_update(
+        encoder_weight, encoder_first, encoder_second, encoder_grad.T
+    )
+    decoder_next, decoder_first_next, decoder_second_next = adam_update(
+        decoder_weight, decoder_first, decoder_second, decoder_grad
+    )
+    return (
+        encoder_next,
+        encoder_first_next,
+        encoder_second_next,
+        decoder_next,
+        decoder_first_next,
+        decoder_second_next,
+        encoder_bias_grad.reshape(-1),
+        decoder_bias_grad.reshape(-1),
+    )
+
+
 def solution(mesh):
     return jax.shard_map(
-        on_device,
+        gathered_step if mesh.shape["lat"] <= 8 and mesh.shape["row"] == 2 else routed_step,
         mesh=mesh,
         in_specs=(
             P(("groups", "lat"), "row"),

time: 355 us -> 137 us (0.39)
  blocking collectives: 152 us -> 0 us
  Pallas kernels: 0 us -> 122 us
  waiting for transfers between devices: 117 us -> 0 us
  local copies, waits for them, and re-layouts: 29.7 us -> 9.9 us
  matrix products: 17.9 us -> 0 us
  between operations: 14.2 us -> 0.73 us
  starting transfers between devices: 9.74 us -> 0 us
  other arithmetic: 12.6 us -> 3.59 us
    pallas_call x0 -> x1, Pallas kernels: none -> 122 us  [gathered_step(): pl.pallas_call(functools.partial(step_kernel, lat_count, loss_scale), out...]
    all_to_all x1 -> x0, blocking collectives: 76.8 us -> none  [on_device(): lax.all_to_all(outgoing, 'lat', split_axis=0, concat_axis=0, tiled=True)]
    psum x1 -> x0, blocking collectives: 75.4 us -> none  [on_device(): decoder_bias_grad = lax.psum(loss_scale * jnp.sum(residual, axis=0), 'lat')]
    all_to_all x2 -> x0, waiting for transfers between devices: 70.7 us -> none  [the longest x1 70.7 us: on_device(): lax.all_to_all(portion.reshape(lat_count, capacity, width_part), 'lat', s...]
    psum x2 -> x0, waiting for transfers between devices: 46.3 us -> none  [the longest x1 25.2 us: on_device(): preact = lax.psum(preact_part, 'row') + encoder_bias]
    dot_general x5 -> x0, matrix products: 17.9 us -> none  [the longest x2 9.33 us: contract_rows(): lax.dot_general(left, right, (((0,), (0,)), ((), ())), preferred_element_...]
    gather x3 -> x0, local copies, waits for them, and re-layouts: 14.8 us -> none  [the longest x1 7.45 us: on_device(): stream_rows[slot_row] * slot_live[:, None]]
    all_to_all x2 -> x0, starting transfers between devices: 9.7 us -> none  [the longest x1 5.27 us: on_device(): lax.all_to_all(portion.reshape(lat_count, capacity, width_part), 'lat', s...]
  transfers between devices with their start and end apart: 4 -> 0, of which waited for: 3 -> 0; matrix products, arithmetic and copies ran while one was open for 1% -> 0% of each run, Pallas kernels for 0% -> 0%
where the time goes in v2:
time: 137 us
  Pallas kernels  122 us (89%)
  local copies, waits for them, and re-layouts  9.9 us (7%)
  other arithmetic  3.59 us (3%)
    pallas_call x1, Pallas kernels, gathered_step(): pl.pallas_call(functools.partial(step_kernel, lat_count, loss_scale), out...  122 us
    unnamed x30, local copies, waits for them, and re-layouts  9.89 us
    convert_element_type x2, other arithmetic, adam_update(): second_next.astype(jnp.bfloat16)  3.58 us

profile of v2, /device:TPU:1, one launch (start us, length us, event | category | flops | bytes accessed | tf_op | source)
XLA Modules:
  0.0 136.5 jit_solution(1515531226510731097)
XLA Ops:
  0.6 0.0 copy-start.10
  0.6 0.7 copy-done.10
  1.3 0.0 copy-start.7
  1.4 1.3 copy.26
  2.7 0.0 copy-done.7
  2.7 0.0 copy-start
  2.7 0.0 copy-start.3
  2.7 0.0 copy-start.4
  2.7 1.0 copy.27
  3.7 0.0 copy-done
  3.7 1.0 copy.25
  4.8 0.0 copy-done.3
  4.8 0.0 copy-done.1
  4.8 0.3 copy-done.2
  5.1 122.3 %shard_map.161 = (f32[128,2048]{1,0:T(8,128)S(1)}, f32[128,2048]{1,0:T(8,128)S(1)}, f32[1,128]{1,0:T(1,128)S(1)}, f32[1,2048]{1,0:T(1,128)S(1)}) custom-call(bf16[128,2048]{1,0:T(8,128)(2,1)S(1)} %copy-done.2, bf16[8,16,128]{2,1,0:T(8,128)(2,1)S(1)} %broadcast_in_dim.2.mask_ref, bf16[2048,128]{1,0:T(8,128)(2,1)S(1)} %copy-done, f32[1,128]{1,0:T(1,128)S(1)} %bitcast.19, ...), custom_call_target="tpu_custom_call" | custom-call | tf_op jit(solution)/shard_map/pallas_call | solution.py:458
  127.4 1.6 %fusion.6 = (bf16[2048,128]{0,1:T(8,128)(2,1)}, bf16[2048,128]{0,1:T(8,128)(2,1)S(1)}, bf16[2048,128]{0,1:T(8,128)(2,1)S(1)}) fusion(f32[128,2048]{1,0:T(8,128)S(1)} %get-tuple-element.12, bf16[2048,128]{0,1:T(8,128)(2,1)S(1)} %copy-done.5, bf16[2048,128]{0,1:T(8,128)(2,1)S(1)} %copy.26, bf16[2048,128]{0,1:T(8,128)(2,1)S(1)} %copy-done.6), kind=kLoop, calls=%fused_computation.12 | loop fusion | flops 4456448 | bytes 4194304 | tf_op jit(solution)/shard_map/convert_element_type | solution.py:26
  129.0 2.0 %copy.30 = bf16[2048,128]{1,0:T(8,128)(2,1)} copy(bf16[2048,128]{0,1:T(8,128)(2,1)} %get-tuple-element.35) | data formatting | bytes 1048576
  131.1 1.0 copy.28
  132.1 1.0 copy.29
  133.1 0.0 copy-done.8
  133.1 0.3 copy-done.9
  133.4 2.0 %fusion.5 = (bf16[128,2048]{1,0:T(8,128)(2,1)}, bf16[128,2048]{1,0:T(8,128)(2,1)}, bf16[128,2048]{1,0:T(8,128)(2,1)}) fusion(f32[128,2048]{1,0:T(8,128)S(1)} %get-tuple-element.13, bf16[128,2048]{1,0:T(8,128)(2,1)S(1)} %copy-done.8, bf16[128,2048]{1,0:T(8,128)(2,1)S(1)} %copy-done.9, bf16[128,2048]{1,0:T(8,128)(2,1)S(1)} %copy-done.1), kind=kLoop, calls=%fused_computation.11 | loop fusion | flops 4456448 | bytes 4194304 | tf_op jit(solution)/shard_map/convert_element_type | solution.py:26
  135.4 0.5 copy.33
  135.9 0.6 copy.34
  (12 shorter events, 0.0 us)
Async XLA Ops:
  0.6 0.7 copy-start.10
  1.3 1.3 copy-start.7
  2.7 1.0 copy-start
  2.7 2.1 %copy-start.3 = (f32[2048]{0:T(1024)S(1)}, f32[2048]{0:T(1024)}, u32[]{:S(2)}) copy-start(f32[2048]{0:T(1024)} %param.15) | copy-start | bytes 24580
  2.7 2.1 %copy-start.4 = (f32[128]{0:T(128)S(1)}, f32[128]{0:T(128)}, u32[]{:S(2)}) copy-start(f32[128]{0:T(128)} %param.13) | copy-start | bytes 1540
  3.7 1.0 copy-start.1
  3.7 1.3 copy-start.2
  5.1 122.3 %copy-start.5 = (bf16[2048,128]{0,1:T(8,128)(2,1)S(1)}, bf16[2048,128]{0,1:T(8,128)(2,1)}, u32[]{:S(2)}) copy-start(bf16[2048,128]{0,1:T(8,128)(2,1)} %copy.27) | copy-start | bytes 1572868
  5.1 122.4 %copy-start.6 = (bf16[2048,128]{0,1:T(8,128)(2,1)S(1)}, bf16[2048,128]{0,1:T(8,128)(2,1)}, u32[]{:S(2)}) copy-start(bf16[2048,128]{0,1:T(8,128)(2,1)} %copy.25) | copy-start | bytes 1572868
  132.1 1.0 copy-start.8
  132.1 1.4 %copy-start.9 = (bf16[128,2048]{1,0:T(8,128)(2,1)S(1)}, bf16[128,2048]{1,0:T(8,128)(2,1)}, u32[]{:S(2)}) copy-start(bf16[128,2048]{1,0:T(8,128)(2,1)} %param.18) | copy-start | bytes 1572868

commit v3 on v2

--- a/solution.py
+++ b/solution.py
@@ -396,7 +396,9 @@
     lows = jnp.concatenate(lows, axis=1)
     for at in range(0, width, TILE):
         cols = slice(at, at + TILE)
-        enc_grad_ref[:, cols] = jnp.dot(lows, rows_all[:, cols], preferred_element_type=jnp.float32)
+        enc_grad_ref[cols, :] = jnp.dot(
+            lows, rows_all[:, cols], preferred_element_type=jnp.float32
+        ).T
     for owner in range(lat_count):
         @pl.when(owner != me)
         def _():
@@ -458,7 +460,7 @@
     encoder_grad, decoder_grad, encoder_bias_grad, decoder_bias_grad = pl.pallas_call(
         functools.partial(step_kernel, lat_count, loss_scale),
         out_shape=(
-            jax.ShapeDtypeStruct((block, width), full),
+            jax.ShapeDtypeStruct((width, block), full),
             jax.ShapeDtypeStruct((block, width), full),
             jax.ShapeDtypeStruct((1, block), full),
             jax.ShapeDtypeStruct((1, width), full),
@@ -497,7 +499,7 @@
         decoder_bias.reshape(1, width),
     )
     encoder_next, encoder_first_next, encoder_second_next = adam_update(
-        encoder_weight, encoder_first, encoder_second, encoder_grad.T
+        encoder_weight, encoder_first, encoder_second, encoder_grad
     )
     decoder_next, decoder_first_next, decoder_second_next = adam_update(
         decoder_weight, decoder_first, decoder_second, decoder_grad

time: 137 us -> 133 us (0.971)
  local copies, waits for them, and re-layouts: 9.9 us -> 5.6 us
    unnamed x30 -> x22, local copies, waits for them, and re-layouts: 9.89 us -> 5.6 us
where the time goes in v3:
time: 133 us
  Pallas kernels  122 us (92%)
  local copies, waits for them, and re-layouts  5.6 us (4%)
  other arithmetic  3.98 us (3%)
    pallas_call x1, Pallas kernels, gathered_step(): pl.pallas_call(functools.partial(step_kernel, lat_count, loss_scale), out...  122 us
    unnamed x22, local copies, waits for them, and re-layouts  5.6 us
    convert_element_type x2, other arithmetic, adam_update(): second_next.astype(jnp.bfloat16)  3.97 us

profile of v3, /device:TPU:1, one launch (start us, length us, event | category | flops | bytes accessed | tf_op | source)
XLA Modules:
  0.0 132.6 jit_solution(4036331330271085076)
XLA Ops:
  0.6 0.0 copy-start.9
  0.6 0.7 copy-done.9
  1.3 0.0 copy-start.3
  1.3 0.0 copy-start.4
  1.4 0.7 copy-done.3
  2.0 0.0 copy-done.4
  2.0 0.0 copy-start
  2.0 1.0 copy-done
  3.1 0.0 copy-start.1
  3.1 1.0 copy-done.1
  4.1 0.0 copy-start.2
  4.1 1.0 copy-done.2
  5.2 0.0 copy-start.5
  5.2 122.3 %shard_map.161 = (f32[2048,128]{1,0:T(8,128)S(1)}, f32[128,2048]{1,0:T(8,128)S(1)}, f32[1,128]{1,0:T(1,128)S(1)}, f32[1,2048]{1,0:T(1,128)S(1)}) custom-call(bf16[128,2048]{1,0:T(8,128)(2,1)S(1)} %copy-done.2, bf16[8,16,128]{2,1,0:T(8,128)(2,1)S(1)} %broadcast_in_dim.2.mask_ref, bf16[2048,128]{1,0:T(8,128)(2,1)S(1)} %copy-done, f32[1,128]{1,0:T(1,128)S(1)} %bitcast.6, ...), custom_call_target="tpu_custom_call" | custom-call | tf_op jit(solution)/shard_map/pallas_call | solution.py:460
  127.5 0.0 copy-done.5
  127.5 0.0 copy-done.6
  127.5 0.0 copy-start.7
  127.5 0.0 copy-start.8
  127.5 2.0 %fusion.5 = (bf16[2048,128]{1,0:T(8,128)(2,1)}, bf16[2048,128]{1,0:T(8,128)(2,1)}, bf16[2048,128]{1,0:T(8,128)(2,1)}) fusion(f32[2048,128]{1,0:T(8,128)S(1)} %get-tuple-element.12, bf16[2048,128]{1,0:T(8,128)(2,1)S(1)} %copy-done.5, bf16[2048,128]{1,0:T(8,128)(2,1)S(1)} %copy-done.6, bf16[2048,128]{1,0:T(8,128)(2,1)S(1)} %copy-done), kind=kLoop, calls=%fused_computation.11 | loop fusion | flops 4456448 | bytes 4194304 | tf_op jit(solution)/shard_map/convert_element_type | solution.py:26
  129.5 0.0 copy-done.7
  129.5 0.0 copy-done.8
  129.5 2.0 %fusion.4 = (bf16[128,2048]{1,0:T(8,128)(2,1)}, bf16[128,2048]{1,0:T(8,128)(2,1)}, bf16[128,2048]{1,0:T(8,128)(2,1)}) fusion(f32[128,2048]{1,0:T(8,128)S(1)} %get-tuple-element.13, bf16[128,2048]{1,0:T(8,128)(2,1)S(1)} %copy-done.7, bf16[128,2048]{1,0:T(8,128)(2,1)S(1)} %copy-done.8, bf16[128,2048]{1,0:T(8,128)(2,1)S(1)} %copy-done.1), kind=kLoop, calls=%fused_computation.10 | loop fusion | flops 4456448 | bytes 4194304 | tf_op jit(solution)/shard_map/convert_element_type | solution.py:26
  131.5 0.5 copy.21
  132.0 0.6 copy.22
  (4 shorter events, 0.0 us)
Async XLA Ops:
  0.6 0.7 copy-start.9
  1.3 0.7 copy-start.3
  1.3 0.7 copy-start.4
  2.0 1.0 copy-start
  3.1 1.0 copy-start.1
  4.1 1.0 copy-start.2
  5.2 122.3 %copy-start.5 = (bf16[2048,128]{1,0:T(8,128)(2,1)S(1)}, bf16[2048,128]{1,0:T(8,128)(2,1)}, u32[]{:S(2)}) copy-start(bf16[2048,128]{1,0:T(8,128)(2,1)} %param.17) | copy-start | bytes 1572868
  5.2 122.4 %copy-start.6 = (bf16[2048,128]{1,0:T(8,128)(2,1)S(1)}, bf16[2048,128]{1,0:T(8,128)(2,1)}, u32[]{:S(2)}) copy-start(bf16[2048,128]{1,0:T(8,128)(2,1)} %param.16) | copy-start | bytes 1572868
  127.5 2.0 %copy-start.7 = (bf16[128,2048]{1,0:T(8,128)(2,1)S(1)}, bf16[128,2048]{1,0:T(8,128)(2,1)}, u32[]{:S(2)}) copy-start(bf16[128,2048]{1,0:T(8,128)(2,1)} %param.19) | copy-start | bytes 1572868
  127.5 2.0 %copy-start.8 = (bf16[128,2048]{1,0:T(8,128)(2,1)S(1)}, bf16[128,2048]{1,0:T(8,128)(2,1)}, u32[]{:S(2)}) copy-start(bf16[128,2048]{1,0:T(8,128)(2,1)} %param.18) | copy-start | bytes 1572868

commit v4 on v3

--- a/solution.py
+++ b/solution.py
@@ -155,6 +155,8 @@
     gather_recv,
     small_send,
     small_recv,
+    enc_here,
+    load_sem,
 ):
     count, width = rows_ref.shape
     chips = lat_count // 2
@@ -166,6 +168,13 @@
     mesh_id = pl.DeviceIdType.MESH
     buffers = (rows_all, dec_all, err_all)
 
+    own = pl.ds(pl.multiple_of(me * count, count), count)
+    load_rows = pltpu.make_async_copy(rows_ref, rows_all.at[own], load_sem.at[0])
+    load_enc = pltpu.make_async_copy(enc_ref, enc_here, load_sem.at[1])
+    load_dec = pltpu.make_async_copy(dec_ref, dec_all.at[own], load_sem.at[2])
+    load_rows.start()
+    load_enc.start()
+    load_dec.start()
     barrier = pltpu.get_barrier_semaphore()
     for step in range(1, lat_count):
         pl.semaphore_signal(
@@ -285,19 +294,20 @@
 
     MASK, PART, CODE, GRAD, GRAD_OUT, SUM = range(6)
 
-    rows_all[span(me)] = rows_ref[...]
+    load_rows.wait()
     for way in range(3):
         own_way(0, way)
     for step in range(1, lat_count):
         target = (me + step) % lat_count
         to_lat(MASK, mask_ref.at[target], masks, target).start()
     masks[me] = mask_ref[me]
-    dec_all[span(me)] = dec_ref[...]
+    load_enc.wait()
+    load_dec.wait()
     own_way(1, 2)
 
     def encode(owner):
         part_mine[owner] = jnp.dot(
-            rows_all[span(owner)], enc_ref[...], preferred_element_type=jnp.float32
+            rows_all[span(owner)], enc_here[...], preferred_element_type=jnp.float32
         )
         across(PART, part_mine, part_other, owner).start()
 
@@ -350,7 +360,7 @@
     for at in range(0, width, TILE):
         cols = slice(at, at + TILE)
         rebuilt = jnp.dot(codes, dec_all[:, cols], preferred_element_type=jnp.float32)
-        residual = rebuilt + dbias_ref[:, cols] - rows_ref[:, cols].astype(jnp.float32)
+        residual = rebuilt + dbias_ref[:, cols] - rows_all[span(me), cols].astype(jnp.float32)
         sums[me, :, cols] = loss_scale * jnp.sum(residual, axis=0, keepdims=True)
         err_all[span(me), cols] = (residual * loss_scale).astype(jnp.bfloat16)
     for way in range(3):
@@ -465,7 +475,9 @@
             jax.ShapeDtypeStruct((1, block), full),
             jax.ShapeDtypeStruct((1, width), full),
         ),
-        in_specs=[pl.BlockSpec(memory_space=pltpu.VMEM)] * 6,
+        in_specs=[
+            pl.BlockSpec(memory_space=pltpu.VMEM if at in (1, 3, 5) else pl.ANY) for at in range(6)
+        ],
         out_specs=[pl.BlockSpec(memory_space=pltpu.VMEM)] * 4,
         scratch_shapes=[
             pltpu.VMEM((everything, width), low),
@@ -486,9 +498,11 @@
             pltpu.SemaphoreType.DMA((3, lat_count, PIECES)),
             pltpu.SemaphoreType.DMA((6, lat_count)),
             pltpu.SemaphoreType.DMA((6, lat_count)),
+            pltpu.VMEM((width, block), low),
+            pltpu.SemaphoreType.DMA((3,)),
         ],
         compiler_params=pltpu.CompilerParams(
-            collective_id=0, has_side_effects=True, vmem_limit_bytes=48 * 1024 * 1024
+            collective_id=0, has_side_effects=True, vmem_limit_bytes=59 * 1024 * 1024
         ),
     )(
         stream_rows,

time: 133 us -> 134 us (level)
  Pallas kernels: 122 us -> 125 us
  local copies, waits for them, and re-layouts: 5.6 us -> 3.11 us
  other arithmetic: 3.98 us -> 5.34 us
    unnamed x22, local copies, waits for them, and re-layouts: 5.6 us -> 2.49 us
    pallas_call x1, Pallas kernels: 122 us -> 125 us  [gathered_step(): pl.pallas_call(functools.partial(step_kernel, lat_count, loss_scale), out...]
    convert_element_type x2, other arithmetic: 3.97 us -> 5.32 us  [adam_update(): second_next.astype(jnp.bfloat16)]
where the time goes in v4:
time: 134 us
  Pallas kernels  125 us (93%)
  other arithmetic  5.34 us (4%)
  local copies, waits for them, and re-layouts  3.11 us (2%)
    pallas_call x1, Pallas kernels, gathered_step(): pl.pallas_call(functools.partial(step_kernel, lat_count, loss_scale), out...  125 us
    convert_element_type x2, other arithmetic, adam_update(): second_next.astype(jnp.bfloat16)  5.32 us

profile of v4, /device:TPU:1, one launch (start us, length us, event | category | flops | bytes accessed | tf_op | source)
XLA Modules:
  0.0 133.7 jit_solution(12326065925890515993)
XLA Ops:
  0.6 0.0 copy-start.8
  0.6 0.7 copy-done.8
  1.3 0.6 broadcast_in_dim.2.mask_ref
  2.0 0.0 copy-start
  2.0 0.0 copy-start.3
  2.0 124.5 %shard_map.161 = (f32[2048,128]{1,0:T(8,128)}, f32[128,2048]{1,0:T(8,128)}, f32[1,128]{1,0:T(1,128)}, f32[1,2048]{1,0:T(1,128)}) custom-call(bf16[128,2048]{1,0:T(8,128)(2,1)} %rows_ref.1, bf16[8,16,128]{2,1,0:T(8,128)(2,1)} %broadcast_in_dim.2.mask_ref, bf16[2048,128]{1,0:T(8,128)(2,1)} %enc_ref.1, f32[1,128]{1,0:T(1,128)} %bitcast.6, ...), custom_call_target="tpu_custom_call" | custom-call | tf_op jit(solution)/shard_map/pallas_call | solution.py:470
  126.5 0.0 copy-done
  126.5 0.0 copy-done.3
  126.5 0.0 copy-done.4
  126.5 0.0 copy-start.1
  126.5 0.0 copy-start.2
  126.5 0.0 copy-start.5
  126.6 0.0 copy-start.6
  126.6 3.3 %fusion.5 = (bf16[2048,128]{1,0:T(8,128)(2,1)}, bf16[2048,128]{1,0:T(8,128)(2,1)}, bf16[2048,128]{1,0:T(8,128)(2,1)}) fusion(f32[2048,128]{1,0:T(8,128)} %get-tuple-element.12, bf16[2048,128]{1,0:T(8,128)(2,1)S(1)} %copy-done.3, bf16[2048,128]{1,0:T(8,128)(2,1)S(1)} %copy-done.4, bf16[2048,128]{1,0:T(8,128)(2,1)S(1)} %copy-done), kind=kLoop, calls=%fused_computation.11 | loop fusion | flops 4456448 | bytes 4194304 | tf_op jit(solution)/shard_map/convert_element_type | solution.py:26
  129.9 0.0 copy-done.1
  129.9 0.0 copy-done.2
  129.9 0.0 copy-done.5
  129.9 0.0 copy-done.6
  129.9 0.0 copy-start.7
  129.9 2.0 %fusion.4 = (bf16[128,2048]{1,0:T(8,128)(2,1)}, bf16[128,2048]{1,0:T(8,128)(2,1)}, bf16[128,2048]{1,0:T(8,128)(2,1)}) fusion(f32[128,2048]{1,0:T(8,128)S(1)} %copy-done.2, bf16[128,2048]{1,0:T(8,128)(2,1)S(1)} %copy-done.5, bf16[128,2048]{1,0:T(8,128)(2,1)S(1)} %copy-done.6, bf16[128,2048]{1,0:T(8,128)(2,1)S(1)} %copy-done.1), kind=kLoop, calls=%fused_computation.10 | loop fusion | flops 4456448 | bytes 4194304 | tf_op jit(solution)/shard_map/convert_element_type | solution.py:26
  131.9 0.7 copy-done.9
  132.6 0.5 copy.21
  133.1 0.0 copy-done.7
  133.1 0.6 copy.22
  (4 shorter events, 0.0 us)
Async XLA Ops:
  0.6 0.7 copy-start.8
  2.0 124.5 %copy-start = (bf16[2048,128]{1,0:T(8,128)(2,1)S(1)}, bf16[2048,128]{1,0:T(8,128)(2,1)}, u32[]{:S(2)}) copy-start(bf16[2048,128]{1,0:T(8,128)(2,1)} %enc_ref.1) | copy-start | bytes 1572868
  2.0 124.5 %copy-start.3 = (bf16[2048,128]{1,0:T(8,128)(2,1)S(1)}, bf16[2048,128]{1,0:T(8,128)(2,1)}, u32[]{:S(2)}) copy-start(bf16[2048,128]{1,0:T(8,128)(2,1)} %param.17) | copy-start | bytes 1572868
  2.0 124.6 %copy-start.4 = (bf16[2048,128]{1,0:T(8,128)(2,1)S(1)}, bf16[2048,128]{1,0:T(8,128)(2,1)}, u32[]{:S(2)}) copy-start(bf16[2048,128]{1,0:T(8,128)(2,1)} %param.16) | copy-start | bytes 1572868
  126.5 3.4 %copy-start.1 = (bf16[128,2048]{1,0:T(8,128)(2,1)S(1)}, bf16[128,2048]{1,0:T(8,128)(2,1)}, u32[]{:S(2)}) copy-start(bf16[128,2048]{1,0:T(8,128)(2,1)} %dec_ref.1) | copy-start | bytes 1572868
  126.5 3.4 %copy-start.2 = (f32[128,2048]{1,0:T(8,128)S(1)}, f32[128,2048]{1,0:T(8,128)}, u32[]{:S(2)}) copy-start(f32[128,2048]{1,0:T(8,128)} %get-tuple-element.13) | copy-start | bytes 3145732
  126.5 3.4 %copy-start.5 = (bf16[128,2048]{1,0:T(8,128)(2,1)S(1)}, bf16[128,2048]{1,0:T(8,128)(2,1)}, u32[]{:S(2)}) copy-start(bf16[128,2048]{1,0:T(8,128)(2,1)} %param.19) | copy-start | bytes 1572868
  126.6 3.4 %copy-start.6 = (bf16[128,2048]{1,0:T(8,128)(2,1)S(1)}, bf16[128,2048]{1,0:T(8,128)(2,1)}, u32[]{:S(2)}) copy-start(bf16[128,2048]{1,0:T(8,128)(2,1)} %param.18) | copy-start | bytes 1572868
  129.9 3.2 %copy-start.7 = (f32[1,2048]{1,0:T(1,128)S(1)}, f32[1,2048]{1,0:T(1,128)}, u32[]{:S(2)}) copy-start(f32[1,2048]{1,0:T(1,128)} %get-tuple-element.15) | copy-start | bytes 24580
  131.9 0.7 copy-start.9
